TPU v7x, 32 devices: a whole 2x2x4 slice. The times are simulated.
32 devices in a mesh: ty: 4 (over x, core), tx: 2 (over y), ta: 4 (over z).
Axes of the slice: x: 2, y: 2, z: 4, core: 2. Of those that a mesh axis runs over, the one named last changes fastest.
Arguments:
- movie: bfloat16 [16, 4, 1024, 256], P('ta', None, 'ty', 'tx'), may hold values from 0 to 2
- footprints: float32 [512, 4096], P(('ty', 'tx')), may hold values from 0 to 1
- traces: float32 [16, 512], P('ta', ('ty', 'tx')), may hold values from 0 to 1
- anchor_row: int32 [512], P(('ty', 'tx')), may hold values from -1 to 15
- anchor_col: int32 [512], P(('ty', 'tx')), may hold values from -1 to 7
Outputs:
- footprints_out: float32 [512, 4096], P(('ty', 'tx'))
- traces_out: float32 [16, 512], P('ta', ('ty', 'tx'))
Inputs may be any that keep to these rules, and one draw needn't show every extreme that they name: `anchor_row`: cell row within the owner tile at which a neuron's patch block starts; -1 puts its upper half into the tile above. `anchor_col`: cell column within the owner tile at which a neuron's patch block starts; -1 puts its left half into the tile beside it.
All inputs are finite; a program needn't handle non-finite values.
Results may differ from a plain program's by a relative error of at most 0.0003.
Values may be sent and summed in bfloat16 or wider, within the bound.
A program may use at most 128 MiB of HBM per device.

v0:
```python
import jax
import jax.numpy as jnp
from jax import lax
from jax.sharding import PartitionSpec as P

CELL = 16
ITERS = 2


RIDGE = 1.0


def with_halo(cells, sides, width):
    for axis, dim in sides:
        count = lax.axis_size(axis)
        ends = count - 1
        head = lax.slice_in_dim(cells, 0, width, axis=dim)
        tail = lax.slice_in_dim(cells, cells.shape[dim] - width, cells.shape[dim], axis=dim)
        cells = jnp.concatenate(
            [
                lax.ppermute(tail, axis, [(i, (i + 1) % count) for i in range(ends)]),
                cells,
                lax.ppermute(head, axis, [((i + 1) % count, i) for i in range(ends)]),
            ],
            axis=dim,
        )
    return cells


def to_cells(movie):
    frames, planes, height, breadth = movie.shape
    cell_rows = height // CELL
    cell_cols = breadth // CELL
    blocks = movie.reshape(frames, planes, cell_rows, CELL, cell_cols, CELL).transpose(
        2, 4, 0, 1, 3, 5
    )
    return blocks.reshape(cell_rows, cell_cols, frames * planes * CELL * CELL)


def fold_rows(extended):
    central = extended[2:-2]
    central = central.at[:2].add(extended[:2])
    return central.at[-2:].add(extended[-2:])


def fold_cols(extended):
    central = extended[:, 2:-2]
    central = central.at[:, :2].add(extended[:, :2])
    return central.at[:, -2:].add(extended[:, -2:])


def combine(partial_value):
    extended = with_halo(partial_value, (("ty", 0), ("tx", 1)), 2)
    return fold_cols(fold_rows(extended))


def patch_residue(observed, footprints, traces, cell_ids, grid_rows, grid_cols):
    owned = footprints.shape[0]
    frames = traces.shape[0]
    shaped = footprints.reshape(owned, 4, 1, -1)
    products = shaped * jnp.transpose(traces)[:, None, :, None]
    partial_value = jax.ops.segment_sum(
        products.reshape(owned * 4, -1), cell_ids, num_segments=grid_rows * grid_cols
    )
    estimate = combine(partial_value.reshape(grid_rows, grid_cols, -1)).reshape(
        grid_rows * grid_cols, frames, -1
    )
    residue = observed - estimate
    return jnp.take(residue, cell_ids, axis=0).reshape(owned, 4, frames, -1)


def shards(movie, footprints, traces, anchor_row, anchor_col):
    owned = footprints.shape[0]
    frames = traces.shape[0]
    local_cells = to_cells(movie)
    grid_rows = local_cells.shape[0] + 2
    grid_cols = local_cells.shape[1] + 2
    rimmed = with_halo(local_cells, (("ty", 0), ("tx", 1)), 1)
    observed = rimmed.reshape(grid_rows * grid_cols, frames, -1).astype(jnp.float32)
    corner = (anchor_row + 1) * grid_cols + anchor_col + 1
    offsets = jnp.array([0, 1, grid_cols, grid_cols + 1], dtype=jnp.int32)
    cell_ids = (corner[:, None] + offsets[None, :]).reshape(-1)
    for sweep in range(ITERS):
        energy = jnp.sum(footprints * footprints, axis=1)
        shaped = footprints.reshape(owned, 4, -1)
        gathered = patch_residue(observed, footprints, traces, cell_ids, grid_rows, grid_cols)
        update = jnp.einsum("kse,ksfe->fk", shaped, gathered, precision=lax.Precision.HIGHEST)
        traces = jnp.maximum(traces + update / (energy + RIDGE)[None, :], 0.0)
        regathered = patch_residue(observed, footprints, traces, cell_ids, grid_rows, grid_cols)
        numer_part = jnp.einsum(
            "fk,ksfe->kse", traces, regathered, precision=lax.Precision.HIGHEST
        ).reshape(owned, -1)
        strength_part = jnp.sum(traces * traces, axis=0)
        numerator, strength = lax.psum((numer_part, strength_part), "ta")
        footprints = jnp.maximum(footprints + numerator / (strength + RIDGE)[:, None], 0.0)
    return (footprints, traces)


def solution(mesh):
    placed = (
        P("ta", None, "ty", "tx"),
        P(("ty", "tx"), None),
        P("ta", ("ty", "tx")),
        P(("ty", "tx")),
        P(("ty", "tx")),
    )
    return jax.shard_map(
        shards,
        mesh=mesh,
        in_specs=placed,
        out_specs=(P(("ty", "tx"), None), P("ta", ("ty", "tx"))),
        check_vma=False,
    )
```

profile of v0, /device:TPU:0, one launch (start us, length us, event | category | flops | bytes accessed | tf_op | source)
XLA Modules:
  0.0 563.2 jit_solution(10692236466892097518)
XLA Ops:
  18.3 8.4 %scatter_custom_fusion = f32[180,4096]{1,0:T(8,128)S(1)} fusion(s32[256]{0:T(256)S(1)} %reshape.627, f32[256,4096]{1,0:T(8,128)} %bitcast.79, f32[]{:T(128)} %constant.364.clone.1), kind=kCustom, calls=%fused_computation.32 | custom fusion | flops 1048576 | bytes 2949632 | tf_op jit(solution)/shard_map/scatter-add | solution.py:62
  34.7 9.5 %reshape.581 = bf16[4,4,16,16,8,16]{5,4,3,2,1,0:T(8,128)(2,1)} reshape(bf16[4,4,256,128]{3,2,1,0:T(8,128)(2,1)} %param.40) | data formatting | bytes 2097152 | tf_op jit(solution)/shard_map/reshape | solution.py:34
  44.2 9.2 %copy.30 = bf16[4,4,16,16,8,16]{5,3,1,0,4,2:T(8,128)(2,1)} copy(bf16[4,4,16,16,8,16]{5,4,3,2,1,0:T(8,128)(2,1)} %reshape.581) | data formatting | bytes 2097152 | tf_op jit(solution)/shard_map/reshape | solution.py:34
  68.3 15.9 %reshape.582 = bf16[16,8,4096]{2,1,0:T(8,128)(2,1)} reshape(bf16[16,8,4,4,16,16]{5,4,3,2,1,0:T(8,128)(2,1)} %bitcast.69) | data formatting | bytes 2097152 | tf_op jit(solution)/shard_map/reshape | solution.py:37
  105.8 7.5 %collective-permute-done.6 = f32[22,2,4096]{2,1,0:T(2,128)S(1)} collective-permute-done((f32[22,2,4096]{2,1,0:T(2,128)S(1)}, f32[22,2,4096]{2,1,0:T(2,128)S(1)}, u32[]{:S(2)}, u32[]{:S(2)}) %collective-permute-start.6) | collective-permute-done | bytes 720928 | tf_op jit(solution)/shard_map/ppermute | solution.py:21
  134.0 6.6 %gather_fusion = f32[256,4,1024]{2,1,0:T(4,128)} fusion(f32[180,4,1024]{2,1,0:T(4,128)} %sub.25, s32[1024]{0:T(1024)S(1)} %pad_clamp_fusion), kind=kCustom, calls=%fused_computation.clone | custom fusion | bytes 8389632 | tf_op jit(solution)/shard_map/jit(_take)/gather | solution.py:69
  143.7 15.2 %fusion.38 = f32[64,1,4,1]{2,1,3,0:T(1,128)S(1)} fusion(f32[64,4,4,1024]{3,2,1,0:T(4,128)S(1)} %bitcast.77, f32[64,4,1024,1]{2,3,1,0:T(1,128)S(1)} %copy-done.15), kind=kOutput, calls=%fused_computation.112 | convolution fusion | flops 12582912 | bytes 5243904 | tf_op jit(solution)/shard_map/kse,ksfe->fk/dot_general | solution.py:87
  167.2 9.2 %scatter_custom_fusion.1 = f32[180,4096]{1,0:T(8,128)} fusion(s32[256]{0:T(256)S(1)} %reshape.627, f32[256,4096]{1,0:T(8,128)} %bitcast.80, f32[]{:T(128)} %constant.364.clone.1), kind=kCustom, calls=%fused_computation.30 | custom fusion | flops 1048576 | bytes 2949632 | tf_op jit(solution)/shard_map/scatter-add | solution.py:62
  198.9 10.9 %collective-permute-done.10 = f32[22,2,4096]{2,1,0:T(2,128)S(1)} collective-permute-done((f32[22,2,4096]{2,1,0:T(2,128)}, f32[22,2,4096]{2,1,0:T(2,128)S(1)}, u32[]{:S(2)}, u32[]{:S(2)}) %collective-permute-start.10) | collective-permute-done | bytes 720928 | tf_op jit(solution)/shard_map/ppermute | solution.py:21
  234.1 6.6 %gather_fusion.1 = f32[256,4,1024]{2,1,0:T(4,128)} fusion(f32[180,4,1024]{2,1,0:T(4,128)} %sub.27, s32[1024]{0:T(1024)S(1)} %pad_clamp_fusion), kind=kCustom, calls=%fused_computation.1.clone | custom fusion | bytes 8389632 | tf_op jit(solution)/shard_map/jit(_take)/gather | solution.py:69
  243.7 7.9 %fusion.39 = f32[64,1,4,1024]{3,1,2,0:T(1,128)S(1)} fusion(f32[4,64,1,1]{0,2,3,1:T(1,128)S(1)} %copy.17, f32[64,4,4,1024]{3,2,1,0:T(4,128)S(1)} %bitcast.71), kind=kOutput, calls=%fused_computation.113 | convolution fusion | flops 12582912 | bytes 5243904 | tf_op jit(solution)/shard_map/fk,ksfe->kse/dot_general | solution.py:90
  253.5 12.3 %psum.29 = f32[64]{0:T(128)S(1)} all-reduce(f32[64]{0:T(128)S(1)} %get-tuple-element.199), channel_id=1, replica_groups=mesh['ty'=4,'tx'=2,'ta'=4] {'ta'}, use_global_device_ids=true, to_apply=%region_5.7 | all-reduce | flops 64 | bytes 512 | tf_op jit(solution)/shard_map/psum | solution.py:94
  265.9 42.8 %all-reduce.3.cloned.1.call-done = f32[64,4096]{1,0:T(8,128)} async-done(((f32[64,4096]{1,0:T(8,128)}), f32[64,4096]{1,0:T(8,128)}) %all-reduce.3.cloned.1.call-update) | async-done | bytes 1048592 | tf_op jit(solution)/shard_map/psum | solution.py:94
  320.0 9.2 %scatter_custom_fusion.2 = f32[180,4096]{1,0:T(8,128)} fusion(s32[256]{0:T(256)S(1)} %reshape.627, f32[256,4096]{1,0:T(8,128)} %bitcast.81, f32[]{:T(128)} %constant.364.clone.1), kind=kCustom, calls=%fused_computation.28 | custom fusion | flops 1048576 | bytes 2949632 | tf_op jit(solution)/shard_map/scatter-add | solution.py:62
  354.9 6.8 %collective-permute-done.14 = f32[22,2,4096]{2,1,0:T(2,128)S(1)} collective-permute-done((f32[22,2,4096]{2,1,0:T(2,128)}, f32[22,2,4096]{2,1,0:T(2,128)S(1)}, u32[]{:S(2)}, u32[]{:S(2)}) %collective-permute-start.14) | collective-permute-done | bytes 720928 | tf_op jit(solution)/shard_map/ppermute | solution.py:21
  378.1 5.9 %sub.29 = f32[180,4,1024]{2,1,0:T(4,128)} reshape(f32[18,10,4096]{2,1,0:T(8,128)} %convert_subtract_fusion.1) | data formatting | bytes 5898240 | tf_op jit(solution)/shard_map/sub | solution.py:68
  383.9 6.6 %gather_fusion.2 = f32[256,4,1024]{2,1,0:T(4,128)} fusion(f32[180,4,1024]{2,1,0:T(4,128)} %sub.29, s32[1024]{0:T(1024)S(1)} %pad_clamp_fusion), kind=kCustom, calls=%fused_computation.2.clone | custom fusion | bytes 8389632 | tf_op jit(solution)/shard_map/jit(_take)/gather | solution.py:69
  393.6 15.2 %fusion.40 = f32[64,1,4,1]{2,1,3,0:T(1,128)S(1)} fusion(f32[64,4,4,1024]{3,2,1,0:T(4,128)S(1)} %bitcast.78, f32[64,4,1024,1]{2,3,1,0:T(1,128)S(1)} %copy-done.16), kind=kOutput, calls=%fused_computation.114 | convolution fusion | flops 12582912 | bytes 5243904 | tf_op jit(solution)/shard_map/kse,ksfe->fk/dot_general | solution.py:87
  415.9 9.2 %scatter_custom_fusion.3 = f32[180,4096]{1,0:T(8,128)} fusion(s32[256]{0:T(256)S(1)} %reshape.627, f32[256,4096]{1,0:T(8,128)} %bitcast.76, f32[]{:T(128)} %constant.364.clone.1), kind=kCustom, calls=%fused_computation.26 | custom fusion | flops 1048576 | bytes 2949632 | tf_op jit(solution)/shard_map/scatter-add | solution.py:62
  426.3 7.4 %collective-permute-start.16 = (f32[2,10,4096]{2,1,0:T(8,128)S(1)}, f32[2,10,4096]{2,1,0:T(8,128)}, u32[]{:S(2)}, u32[]{:S(2)}) collective-permute-start(f32[2,10,4096]{2,1,0:T(8,128)S(1)} %slice.609), channel_id=1, source_target_pairs={{0,8},{8,16},{16,24},{1,9},{9,17},{17,25},{2,10},{10,18},{18,26},{... | collective-permute-start | bytes 983048 | tf_op jit(solution)/shard_map/ppermute | solution.py:21
  451.0 11.2 %collective-permute-done.18 = f32[22,2,4096]{2,1,0:T(2,128)S(1)} collective-permute-done((f32[22,2,4096]{2,1,0:T(2,128)}, f32[22,2,4096]{2,1,0:T(2,128)S(1)}, u32[]{:S(2)}, u32[]{:S(2)}) %collective-permute-start.18) | collective-permute-done | bytes 720928 | tf_op jit(solution)/shard_map/ppermute | solution.py:21
  490.9 7.9 %fusion.41 = f32[64,1,4,1024]{3,1,2,0:T(1,128)S(1)} fusion(f32[4,64,1,1]{0,2,3,1:T(1,128)S(1)} %copy.21, f32[64,4,4,1024]{3,2,1,0:T(4,128)S(1)} %bitcast.70), kind=kOutput, calls=%fused_computation.115 | convolution fusion | flops 12582912 | bytes 5243904 | tf_op jit(solution)/shard_map/fk,ksfe->kse/dot_general | solution.py:90
  500.7 10.2 %psum.31 = f32[64]{0:T(128)S(1)} all-reduce(f32[64]{0:T(128)S(1)} %get-tuple-element.195), channel_id=1, replica_groups=mesh['ty'=4,'tx'=2,'ta'=4] {'ta'}, use_global_device_ids=true, to_apply=%region_11.13 | all-reduce | flops 64 | bytes 512 | tf_op jit(solution)/shard_map/psum | solution.py:94
  510.9 42.7 %all-reduce.5.cloned.1.call-done = f32[64,4096]{1,0:T(8,128)} async-done(((f32[64,4096]{1,0:T(8,128)}), f32[64,4096]{1,0:T(8,128)}) %all-reduce.5.cloned.1.call-update) | async-done | bytes 1048592 | tf_op jit(solution)/shard_map/psum | solution.py:94
  (199 shorter events, 253.6 us)
Async XLA Ops:
  7.2 301.5 %all-reduce.3.cloned.1.call-start = ((), (), s32[]{:S(2)}) async-start(), calls=%async_computation | async-start | bytes 2097152 | tf_op jit(solution)/shard_map/psum | solution.py:94
  29.4 59.4 %collective-permute-start.4 = (f32[2,10,4096]{2,1,0:T(8,128)}, f32[2,10,4096]{2,1,0:T(8,128)}, u32[]{:S(2)}, u32[]{:S(2)}) collective-permute-start(f32[2,10,4096]{2,1,0:T(8,128)} %slice.561), channel_id=1, source_target_pairs={{0,8},{8,16},{16,24},{1,9},{9,17},{17,25},{2,10},{10,18},{18,26},{... | collective-permute-start | bytes 983048 | tf_op jit(solution)/shard_map/ppermute | solution.py:21
  33.5 59.1 %collective-permute-start.5 = (f32[2,10,4096]{2,1,0:T(8,128)}, f32[2,10,4096]{2,1,0:T(8,128)}, u32[]{:S(2)}, u32[]{:S(2)}) collective-permute-start(f32[2,10,4096]{2,1,0:T(8,128)} %slice.563), channel_id=1, source_target_pairs={{8,0},{16,8},{24,16},{9,1},{17,9},{25,17},{10,2},{18,10},{26,18},{... | collective-permute-start | bytes 983048 | tf_op jit(solution)/shard_map/ppermute | solution.py:23
  58.1 28.6 %collective-permute-start = (bf16[1,8,4096]{2,1,0:T(8,128)(2,1)}, bf16[1,8,4096]{2,1,0:T(8,128)(2,1)}, u32[]{:S(2)}, u32[]{:S(2)}) collective-permute-start(bf16[1,8,4096]{2,1,0:T(8,128)(2,1)} %slice.555), channel_id=1, source_target_pairs={{0,8},{8,16},{16,24},{1,9},{9,17},{17,25},{2,10},{10,18},{18,26},{... | collective-permute-start | bytes 196616 | tf_op jit(solution)/shard_map/ppermute | solution.py:21
  64.4 24.4 %collective-permute-start.1 = (bf16[1,8,4096]{2,1,0:T(8,128)(2,1)}, bf16[1,8,4096]{2,1,0:T(8,128)(2,1)S(1)}, u32[]{:S(2)}, u32[]{:S(2)}) collective-permute-start(bf16[1,8,4096]{2,1,0:T(8,128)(2,1)} %slice.557), channel_id=1, source_target_pairs={{8,0},{16,8},{24,16},{9,1},{17,9},{25,17},{10,2},{18,10},{26,18},{... | collective-permute-start | bytes 196616 | tf_op jit(solution)/shard_map/ppermute | solution.py:23
  94.1 19.2 %collective-permute-start.6 = (f32[22,2,4096]{2,1,0:T(2,128)S(1)}, f32[22,2,4096]{2,1,0:T(2,128)S(1)}, u32[]{:S(2)}, u32[]{:S(2)}) collective-permute-start(f32[22,2,4096]{2,1,0:T(2,128)S(1)} %get-tuple-element.209), channel_id=1, source_target_pairs={{0,4},{1,5},{2,6},{3,7},{8,12},{9,13},{10,14},{11,15},{16,20},{17,... | collective-permute-start | bytes 2162696 | tf_op jit(solution)/shard_map/ppermute | solution.py:21
  97.6 20.5 %collective-permute-start.7 = (f32[22,2,4096]{2,1,0:T(2,128)S(1)}, f32[22,2,4096]{2,1,0:T(2,128)S(1)}, u32[]{:S(2)}, u32[]{:S(2)}) collective-permute-start(f32[22,2,4096]{2,1,0:T(2,128)S(1)} %get-tuple-element.210), channel_id=1, source_target_pairs={{4,0},{5,1},{6,2},{7,3},{12,8},{13,9},{14,10},{15,11},{20,16},{21,... | collective-permute-start | bytes 2162696 | tf_op jit(solution)/shard_map/ppermute | solution.py:23
  99.5 22.4 %collective-permute-start.2 = (bf16[18,1,4096]{2,1,0:T(2,128)(2,1)S(1)}, bf16[18,1,4096]{2,1,0:T(2,128)(2,1)S(1)}, u32[]{:S(2)}, u32[]{:S(2)}) collective-permute-start(bf16[18,1,4096]{2,1,0:T(2,128)(2,1)S(1)} %get-tuple-element.219), channel_id=1, source_target_pairs={{0,4},{1,5},{2,6},{3,7},{8,12},{9,13},{10,14},{11,15},{16,20},{17,... | collective-permute-start | bytes 442376 | tf_op jit(solution)/shard_map/ppermute | solution.py:21
  104.1 20.3 %collective-permute-start.3 = (bf16[18,1,4096]{2,1,0:T(2,128)(2,1)S(1)}, bf16[18,1,4096]{2,1,0:T(2,128)(2,1)S(1)}, u32[]{:S(2)}, u32[]{:S(2)}) collective-permute-start(bf16[18,1,4096]{2,1,0:T(2,128)(2,1)S(1)} %get-tuple-element.220), channel_id=1, source_target_pairs={{4,0},{5,1},{6,2},{7,3},{12,8},{13,9},{14,10},{15,11},{20,16},{21,... | collective-permute-start | bytes 442376 | tf_op jit(solution)/shard_map/ppermute | solution.py:23
  121.9 103.2 %copy-start.10 = (bf16[18,1,4096]{2,1,0:T(2,128)(2,1)}, bf16[18,1,4096]{2,1,0:T(2,128)(2,1)S(1)}, u32[]{:S(2)}) copy-start(bf16[18,1,4096]{2,1,0:T(2,128)(2,1)S(1)} %collective-permute-done.2) | copy-start | bytes 442372
  178.4 9.2 %collective-permute-start.8 = (f32[2,10,4096]{2,1,0:T(8,128)}, f32[2,10,4096]{2,1,0:T(8,128)}, u32[]{:S(2)}, u32[]{:S(2)}) collective-permute-start(f32[2,10,4096]{2,1,0:T(8,128)} %slice.577), channel_id=1, source_target_pairs={{0,8},{8,16},{16,24},{1,9},{9,17},{17,25},{2,10},{10,18},{18,26},{... | collective-permute-start | bytes 983048 | tf_op jit(solution)/shard_map/ppermute | solution.py:21
  186.0 5.6 %collective-permute-start.9 = (f32[2,10,4096]{2,1,0:T(8,128)}, f32[2,10,4096]{2,1,0:T(8,128)S(1)}, u32[]{:S(2)}, u32[]{:S(2)}) collective-permute-start(f32[2,10,4096]{2,1,0:T(8,128)} %slice.579), channel_id=1, source_target_pairs={{8,0},{16,8},{24,16},{9,1},{17,9},{25,17},{10,2},{18,10},{26,18},{... | collective-permute-start | bytes 983048 | tf_op jit(solution)/shard_map/ppermute | solution.py:23
  195.7 14.1 %collective-permute-start.10 = (f32[22,2,4096]{2,1,0:T(2,128)}, f32[22,2,4096]{2,1,0:T(2,128)S(1)}, u32[]{:S(2)}, u32[]{:S(2)}) collective-permute-start(f32[22,2,4096]{2,1,0:T(2,128)} %get-tuple-element.207), channel_id=1, source_target_pairs={{0,4},{1,5},{2,6},{3,7},{8,12},{9,13},{10,14},{11,15},{16,20},{17,... | collective-permute-start | bytes 2162696 | tf_op jit(solution)/shard_map/ppermute | solution.py:21
  197.5 17.0 %collective-permute-start.11 = (f32[22,2,4096]{2,1,0:T(2,128)}, f32[22,2,4096]{2,1,0:T(2,128)}, u32[]{:S(2)}, u32[]{:S(2)}) collective-permute-start(f32[22,2,4096]{2,1,0:T(2,128)} %get-tuple-element.208), channel_id=1, source_target_pairs={{4,0},{5,1},{6,2},{7,3},{12,8},{13,9},{14,10},{15,11},{20,16},{21,... | collective-permute-start | bytes 2162696 | tf_op jit(solution)/shard_map/ppermute | solution.py:23
  253.5 300.1 %all-reduce.5.cloned.1.call-start = ((), (), s32[]{:S(2)}) async-start(), calls=%async_computation.1 | async-start | bytes 2097152 | tf_op jit(solution)/shard_map/psum | solution.py:94
  330.5 8.0 %collective-permute-start.12 = (f32[2,10,4096]{2,1,0:T(8,128)S(1)}, f32[2,10,4096]{2,1,0:T(8,128)}, u32[]{:S(2)}, u32[]{:S(2)}) collective-permute-start(f32[2,10,4096]{2,1,0:T(8,128)S(1)} %slice.593), channel_id=1, source_target_pairs={{0,8},{8,16},{16,24},{1,9},{9,17},{17,25},{2,10},{10,18},{18,26},{... | collective-permute-start | bytes 983048 | tf_op jit(solution)/shard_map/ppermute | solution.py:21
  337.2 5.3 collective-permute-start.13
  346.6 15.1 %collective-permute-start.14 = (f32[22,2,4096]{2,1,0:T(2,128)}, f32[22,2,4096]{2,1,0:T(2,128)S(1)}, u32[]{:S(2)}, u32[]{:S(2)}) collective-permute-start(f32[22,2,4096]{2,1,0:T(2,128)} %get-tuple-element.205), channel_id=1, source_target_pairs={{0,4},{1,5},{2,6},{3,7},{8,12},{9,13},{10,14},{11,15},{16,20},{17,... | collective-permute-start | bytes 2162696 | tf_op jit(solution)/shard_map/ppermute | solution.py:21
  350.0 16.4 %collective-permute-start.15 = (f32[22,2,4096]{2,1,0:T(2,128)}, f32[22,2,4096]{2,1,0:T(2,128)}, u32[]{:S(2)}, u32[]{:S(2)}) collective-permute-start(f32[22,2,4096]{2,1,0:T(2,128)} %get-tuple-element.206), channel_id=1, source_target_pairs={{4,0},{5,1},{6,2},{7,3},{12,8},{13,9},{14,10},{15,11},{20,16},{21,... | collective-permute-start | bytes 2162696 | tf_op jit(solution)/shard_map/ppermute | solution.py:23
  426.3 13.4 %collective-permute-start.16 = (f32[2,10,4096]{2,1,0:T(8,128)S(1)}, f32[2,10,4096]{2,1,0:T(8,128)}, u32[]{:S(2)}, u32[]{:S(2)}) collective-permute-start(f32[2,10,4096]{2,1,0:T(8,128)S(1)} %slice.609), channel_id=1, source_target_pairs={{0,8},{8,16},{16,24},{1,9},{9,17},{17,25},{2,10},{10,18},{18,26},{... | collective-permute-start | bytes 983048 | tf_op jit(solution)/shard_map/ppermute | solution.py:21
  438.3 5.5 collective-permute-start.17
  447.8 14.4 %collective-permute-start.18 = (f32[22,2,4096]{2,1,0:T(2,128)}, f32[22,2,4096]{2,1,0:T(2,128)S(1)}, u32[]{:S(2)}, u32[]{:S(2)}) collective-permute-start(f32[22,2,4096]{2,1,0:T(2,128)} %get-tuple-element.203), channel_id=1, source_target_pairs={{0,4},{1,5},{2,6},{3,7},{8,12},{9,13},{10,14},{11,15},{16,20},{17,... | collective-permute-start | bytes 2162696 | tf_op jit(solution)/shard_map/ppermute | solution.py:21
  449.6 17.2 %collective-permute-start.19 = (f32[22,2,4096]{2,1,0:T(2,128)}, f32[22,2,4096]{2,1,0:T(2,128)S(1)}, u32[]{:S(2)}, u32[]{:S(2)}) collective-permute-start(f32[22,2,4096]{2,1,0:T(2,128)} %get-tuple-element.204), channel_id=1, source_target_pairs={{4,0},{5,1},{6,2},{7,3},{12,8},{13,9},{14,10},{15,11},{20,16},{21,... | collective-permute-start | bytes 2162696 | tf_op jit(solution)/shard_map/ppermute | solution.py:23
  490.8 62.7 %copy-start.6 = (f32[64,4096]{1,0:T(8,128)S(1)}, f32[64,4096]{1,0:T(8,128)}, u32[]{:S(2)}) copy-start(f32[64,4096]{1,0:T(8,128)} %get-tuple-element.198) | copy-start | bytes 3145732
  (19 other events, 163.4 us)
Sparse Core Ops, SparseCore 0:
  253.6 54.9 all-reduce.2
  500.8 52.7 all-reduce.4
where the time goes:
time: 574 us; the launch traced here: 563 us
  local copies, waits for them, and re-layouts  188 us (33%)
  waiting for transfers between devices  143 us (25%)
  other arithmetic  97.1 us (17%)
  starting transfers between devices  50.5 us (9%)
  matrix products  46.2 us (8%)
  blocking collectives  22.5 us (4%)
  between operations  15.3 us (3%)
    psum x2, waiting for transfers between devices, shards(): numerator, strength = lax.psum((numer_part, strength_part), 'ta')  85.5 us
    unnamed x58, local copies, waits for them, and re-layouts  56.6 us
    ppermute x10, starting transfers between devices, with_halo(): lax.ppermute(tail, axis, [(i, (i + 1) % count) for i in range(ends)])  36.5 us
    ppermute x10, waiting for transfers between devices, with_halo(): lax.ppermute(tail, axis, [(i, (i + 1) % count) for i in range(ends)])  36.4 us
    scatter-add x4, other arithmetic, patch_residue(): jax.ops.segment_sum(products.reshape(owned * 4, -1), cell_ids, num_segmen...  36.2 us
    dot_general x2, matrix products, shards(): jnp.einsum('kse,ksfe->fk', shaped, gathered, precision=lax.Precision.HIGH...  30.3 us
    gather x4, local copies, waits for them, and re-layouts, patch_residue(): return jnp.take(residue, cell_ids, axis=0).reshape(owned, 4, frames, -1)  24.4 us
    psum x2, blocking collectives, shards(): numerator, strength = lax.psum((numer_part, strength_part), 'ta')  22.5 us
  transfers between devices with their start and end apart: 22, of which 11 were waited for; matrix products, arithmetic and copies ran while one was open for 15% of the time, Pallas kernels for 0%

commit v1 on v0

v1 whole, which is shorter than its diff:
```python
import functools

import jax
import jax.numpy as jnp
from jax import lax
from jax.experimental import pallas as pl
from jax.experimental.pallas import tpu as pltpu
from jax.sharding import PartitionSpec as P

CELL = 16
ITERS = 2
RIDGE = 1.0
HI = lax.Precision.HIGHEST
F32 = jnp.float32
BF16 = jnp.bfloat16
MESH = pl.DeviceIdType.MESH


def reach(count):
    return [0] if count == 1 else [0, 1] if count == 2 else [0, -1, 1]


def directions(mesh_y, mesh_x):
    return [(dy, dx) for dy in reach(mesh_y) for dx in reach(mesh_x)]


def shift(at, count, d):
    if d == 0:
        return at, None
    if count == 2:
        return 1 - at, None
    to = at + d
    return to, (to >= 0) & (to < count)


def opposite(d, count):
    return d if count == 2 else -d


def thirds(x):
    high = x.astype(BF16)
    rest = x - high.astype(F32)
    middle = rest.astype(BF16)
    return high, middle, (rest - middle.astype(F32)).astype(BF16)


def nt(a, b):
    return lax.dot_general(a, b, (((1,), (1,)), ((), ())), precision=HI, preferred_element_type=F32)


def nn(a, b):
    return jnp.dot(a, b, precision=HI, preferred_element_type=F32)


def kernel(
    sizes, movie, foot, trace, idrow, idcol, place, placerow,
    foot_out, trace_out,
    seen, cut, patch, foot_at, info_at, times_at, trace_at, part_at, feet_t, numer,
    s_mov, r_mov, s_cut, r_cut, s_foot, r_foot, s_tr, r_tr, s_info, r_info,
    s_time, r_time, s_part, r_part, s_out, r_out, l_sem,
):
    ny, nx, nz, rows, cols, local, planes, owned = sizes
    frames = local * nz
    spot = CELL * CELL
    lanes = 4 * owned
    strip = cut.shape[2]
    iy, ix, iz = lax.axis_index("ty"), lax.axis_index("tx"), lax.axis_index("ta")
    dirs = directions(ny, nx)
    slots = len(dirs)

    near = []
    for j, (dy, dx) in enumerate(dirs):
        ty, ey = shift(iy, ny, dy)
        tx, ex = shift(ix, nx, dx)
        exists = ey if ex is None else ex if ey is None else ey & ex
        back = dirs.index((opposite(dy, ny), opposite(dx, nx)))
        near.append(((ty, tx, iz), exists, back))

    def when(exists, act):
        if exists is None:
            act()
        else:
            pl.when(exists)(act)

    def far(o):
        return (iy, ix, lax.rem(iz + o, nz))

    def spread(src, dst, ssem, rsem):
        def go(j):
            device, exists, back = near[j]
            when(exists, lambda: pltpu.make_async_remote_copy(
                src_ref=src(j), dst_ref=dst(back), send_sem=ssem.at[j], recv_sem=rsem.at[back],
                device_id=device, device_id_type=MESH).start())
        for j in range(1, slots):
            go(j)

    def await_near(j, dst, ssem, rsem, send=False):
        device, exists, _ = near[j]

        def act():
            copy = pltpu.make_async_remote_copy(
                src_ref=dst, dst_ref=dst, send_sem=ssem.at[j], recv_sem=rsem.at[j],
                device_id=device, device_id_type=MESH)
            copy.wait_send() if send else copy.wait_recv()

        when(exists, act)

    def to_far(o, src, dst, ssem, rsem):
        return pltpu.make_async_remote_copy(
            src_ref=src, dst_ref=dst, send_sem=ssem, recv_sem=rsem,
            device_id=far(o), device_id_type=MESH)

    barrier = pltpu.get_barrier_semaphore()
    due = jnp.int32(nz - 1)
    for o in range(1, nz):
        pl.semaphore_signal(barrier, inc=1, device_id=far(o), device_id_type=MESH)
    for j in range(1, slots):
        device, exists, _ = near[j]
        when(exists, lambda device=device: pl.semaphore_signal(
            barrier, inc=1, device_id=device, device_id_type=MESH))
        due = due + (1 if exists is None else exists.astype(jnp.int32))
    pl.semaphore_wait(barrier, due)

    for o in range(1, nz):
        to_far(o, trace, trace_at.at[iz], s_tr.at[o], r_tr.at[o]).start()
    for o in range(1, nz):
        to_far(o, movie.at[lax.rem(iz + o, nz)], seen.at[pl.ds(iz * local, local)],
               s_mov.at[o], r_mov.at[o]).start()
    own = pltpu.make_async_copy(movie.at[iz], seen.at[pl.ds(iz * local, local)], l_sem)
    own.start()
    trace_at[iz] = trace[...]
    for s in range(4):
        first = pl.multiple_of((s * planes + iz) * spot, spot)
        foot_at[0, 0, s * owned:(s + 1) * owned, :] = foot[:, pl.ds(first, spot)]
    spread(lambda j: foot_at.at[0, 0], lambda b: foot_at.at[0, b], s_foot.at[0], r_foot.at[0])

    for j in range(1, slots):
        _, exists, _ = near[j]
        if exists is not None:
            def clear(j=j):
                for n in range(ITERS):
                    foot_at[n, j] = jnp.zeros_like(foot_at[n, j])
                for n in range(ITERS):
                    times_at[n, j] = jnp.zeros_like(times_at[n, j])
                info_at[j] = jnp.zeros_like(info_at[j])
                cut[j] = jnp.zeros_like(cut[j])
            pl.when(jnp.logical_not(exists))(clear)

    for o in range(1, nz):
        back = lax.rem(iz + nz - o, nz)
        to_far(o, trace, trace_at.at[back], s_tr.at[o], r_tr.at[o]).wait_recv()
    pad = trace.shape[0]
    r = lax.broadcasted_iota(jnp.int32, (frames, nz * pad), 0)
    c = lax.broadcasted_iota(jnp.int32, (frames, nz * pad), 1)
    pick = ((r // local == c // pad) & (r % local == c % pad)).astype(F32)
    t = nn(pick, trace_at[...].reshape(nz * pad, lanes))
    info_at[0, 0:frames, :] = t
    info_at[0, frames:frames + 8, :] = idrow[...]
    spread(lambda j: info_at.at[0], lambda b: info_at.at[b], s_info, r_info)

    gather = (idcol[...] == placerow[0:1, :]).astype(BF16)
    a = lax.broadcasted_iota(jnp.int32, (lanes, lanes), 0)
    b = lax.broadcasted_iota(jnp.int32, (lanes, lanes), 1)
    fold = (a % owned == b % owned).astype(F32)
    central = rows * cols

    for n in range(ITERS):
        feet = foot_at[n, 0]
        update = jnp.zeros((frames, lanes), F32)
        same = []
        for j in range(slots):
            if n == 0 and j:
                await_near(j, info_at.at[j], s_info, r_info)
            if j:
                await_near(j, foot_at.at[n, j], s_foot.at[n], r_foot.at[n])
            same.append(idcol[...] == info_at[j, frames:frames + 1, :])
            tj = info_at[j, 0:frames, :] if n == 0 else times_at[n - 1, j]
            over = jnp.where(same[j], nt(feet, foot_at[n, j]), 0.0)
            update = update - nt(tj, over)
        if n == 0:
            own.wait()
            for o in range(1, nz):
                back = lax.rem(iz + nz - o, nz)
                to_far(o, movie.at[iz], seen.at[pl.ds(back * local, local)],
                       s_mov.at[o], r_mov.at[o]).wait_recv()
            for j, (dy, dx) in enumerate(dirs):
                if j == 0:
                    continue
                if dy:
                    start = 0 if dy < 0 else central - strip
                    if ny == 2:
                        start = jnp.where(iy == 0, central - strip, 0)
                    u = lax.broadcasted_iota(jnp.int32, (strip, central), 0) + start
                else:
                    column = 0 if dx < 0 else cols - 1
                    if nx == 2:
                        column = jnp.where(ix == 0, cols - 1, 0)
                    u = lax.broadcasted_iota(jnp.int32, (strip, central), 0) * cols + column
                v = lax.broadcasted_iota(jnp.int32, (strip, central), 1)
                choose = (u == v).astype(BF16)

                def body(f, carry, j=j, choose=choose):
                    cut[slots + j, f] = jnp.dot(
                        choose, seen[f], preferred_element_type=F32).astype(BF16)
                    return carry
                lax.fori_loop(0, frames, body, 0)
            spread(lambda j: cut.at[slots + j], lambda b: cut.at[b], s_cut, r_cut)
            for j in range(1, slots):
                await_near(j, cut.at[j], s_cut, r_cut)

            def collect(f, carry):
                got = jnp.dot(gather[:, 0:central], seen[f], preferred_element_type=F32)
                for j in range(1, slots):
                    at = central + (j - 1) * strip
                    got = got + jnp.dot(
                        gather[:, at:at + strip], cut[j, f], preferred_element_type=F32)
                patch[f] = got
                return carry
            lax.fori_loop(0, frames, collect, 0)
        energy = nt(jnp.ones((8, spot), F32), feet * feet)

        feet_t[...] = feet

        def inner(f, carry):
            numer[pl.ds(f, 1), :] = jnp.sum(
                jnp.transpose(feet_t[...] * patch[f]), axis=0, keepdims=True)
            return carry
        lax.fori_loop(0, frames, inner, 0)
        part_at[n, iz, 0:frames, :] = update + numer[...]
        part_at[n, iz, frames:frames + 8, :] = energy
        for o in range(1, nz):
            to_far(o, part_at.at[n, iz], part_at.at[n, iz], s_part.at[n, o], r_part.at[n, o]).start()
        for o in range(1, nz):
            back = lax.rem(iz + nz - o, nz)
            to_far(o, part_at.at[n, iz], part_at.at[n, back],
                   s_part.at[n, o], r_part.at[n, o]).wait_recv()
        total = part_at[n, 0]
        for z in range(1, nz):
            total = total + part_at[n, z]
        total = nn(total, fold)
        t = jnp.maximum(t + total[0:frames] / (total[frames:frames + 1] + RIDGE), 0.0)
        times_at[n, 0] = t
        spread(lambda j: times_at.at[n, 0], lambda b: times_at.at[n, b], s_time.at[n], r_time.at[n])
        wide = jnp.concatenate([t, jnp.zeros((128 - frames, lanes), F32)], axis=0)
        cols_t = jnp.transpose(wide)
        strength = jnp.sum(cols_t * cols_t, axis=1, keepdims=True)
        total_n = jnp.zeros((lanes, spot), F32)
        for f in range(frames):
            total_n = total_n + cols_t[:, f:f + 1] * patch[f]
        for j in range(slots):
            if j:
                await_near(j, times_at.at[n, j], s_time.at[n], r_time.at[n])
            both = jnp.where(same[j], nn(cols_t[:, 0:frames], times_at[n, j]), 0.0)
            total_n = total_n - nn(both, foot_at[n, j])
        feet = jnp.maximum(feet + total_n / (strength + RIDGE), 0.0)
        foot_at[n + 1, 0] = feet
        if n + 1 < ITERS:
            spread(lambda j: foot_at.at[n + 1, 0], lambda b: foot_at.at[n + 1, b],
                   s_foot.at[n + 1], r_foot.at[n + 1])

    trace_out[...] = t

    def block(o, s, z):
        first = pl.multiple_of((s * planes + z) * spot, spot)
        return to_far(o, foot_at.at[ITERS, 0, pl.ds(s * owned, owned)],
                      foot_out.at[:, pl.ds(first, spot)], s_out.at[o, s], r_out.at[o, s])

    for o in range(1, nz):
        for s in range(4):
            block(o, s, iz).start()
    for s in range(4):
        first = pl.multiple_of((s * planes + iz) * spot, spot)
        foot_out[:, pl.ds(first, spot)] = foot_at[ITERS, 0, s * owned:(s + 1) * owned, :]
    for o in range(1, nz):
        for s in range(4):
            block(o, s, lax.rem(iz + nz - o, nz)).wait_recv()
    for o in range(1, nz):
        to_far(o, trace, trace_at.at[iz], s_tr.at[o], r_tr.at[o]).wait_send()
        to_far(o, movie.at[iz], seen.at[pl.ds(iz * local, local)], s_mov.at[o], r_mov.at[o]).wait_send()
        for n in range(ITERS):
            to_far(o, part_at.at[n, iz], part_at.at[n, iz], s_part.at[n, o], r_part.at[n, o]).wait_send()
        for s in range(4):
            block(o, s, iz).wait_send()
    for j in range(1, slots):
        await_near(j, info_at.at[0], s_info, r_info, True)
        await_near(j, cut.at[slots + j], s_cut, r_cut, True)
        for n in range(ITERS):
            await_near(j, foot_at.at[n, 0], s_foot.at[n], r_foot.at[n], True)
            await_near(j, times_at.at[n, 0], s_time.at[n], r_time.at[n], True)


def shards(movie, footprints, traces, anchor_row, anchor_col):
    owned = footprints.shape[0]
    local, planes, height, breadth = movie.shape
    rows, cols = height // CELL, breadth // CELL
    spot = CELL * CELL
    ny, nx, nz = (lax.axis_size(a) for a in ("ty", "tx", "ta"))
    assert planes == nz
    frames, lanes = local * nz, 4 * owned
    cells = movie.reshape(local, planes, rows, CELL, cols, CELL).transpose(1, 0, 2, 4, 3, 5)
    cells = cells.reshape(planes, local, rows * cols, spot)
    width = cols * nx + 2
    iy, ix = lax.axis_index("ty"), lax.axis_index("tx")
    first = (anchor_row + 1 + iy * rows) * width + anchor_col + 1 + ix * cols
    offsets = jnp.array([0, 1, width, width + 1], dtype=jnp.int32)
    ids = (offsets[:, None] + first[None, :]).reshape(-1).astype(F32)
    strip = rows
    dirs = directions(ny, nx)
    slots = len(dirs)
    places = []
    for j, (dy, dx) in enumerate(dirs):
        ty = 1 - iy if dy and ny == 2 else iy + dy
        tx = 1 - ix if dx and nx == 2 else ix + dx
        if j == 0:
            within = jnp.arange(rows * cols)
        elif dy:
            below = (iy == 0) if ny == 2 else dy > 0
            within = jnp.arange(strip) + jnp.where(below, 0, rows * cols - strip)
        else:
            right = (ix == 0) if nx == 2 else dx > 0
            within = jnp.arange(strip) * cols + jnp.where(right, 0, cols - 1)
        places.append(
            (ty * rows + within // cols + 1) * width + tx * cols + within % cols + 1)
    place = jnp.concatenate(places).astype(F32)
    pad = -(-local // 8) * 8
    marks = jnp.zeros((pad, lanes), F32).at[:local].set(jnp.tile(traces, (1, 4)))
    dma = pltpu.SemaphoreType.DMA
    feet, marks = pl.pallas_call(
        functools.partial(kernel, (ny, nx, nz, rows, cols, local, planes, owned)),
        out_shape=(
            jax.ShapeDtypeStruct(footprints.shape, F32),
            jax.ShapeDtypeStruct((frames, lanes), F32),
        ),
        in_specs=[pl.BlockSpec(memory_space=pltpu.VMEM)] * 7,
        out_specs=[pl.BlockSpec(memory_space=pltpu.VMEM)] * 2,
        scratch_shapes=[
            pltpu.VMEM((frames, rows * cols, spot), BF16),
            pltpu.VMEM((2 * slots, frames, strip, spot), BF16),
            pltpu.VMEM((frames, lanes, spot), F32),
            pltpu.VMEM((ITERS + 1, slots, lanes, spot), F32),
            pltpu.VMEM((slots, frames + 8, lanes), F32),
            pltpu.VMEM((ITERS, slots, frames, lanes), F32),
            pltpu.VMEM((nz, pad, lanes), F32),
            pltpu.VMEM((ITERS, nz, frames + 8, lanes), F32),
            pltpu.VMEM((lanes, spot), F32),
            pltpu.VMEM((frames, lanes), F32),
            dma((nz,)), dma((nz,)),
            dma((slots,)), dma((slots,)),
            dma((ITERS, slots)), dma((ITERS, slots)),
            dma((nz,)), dma((nz,)),
            dma((slots,)), dma((slots,)),
            dma((ITERS, slots)), dma((ITERS, slots)),
            dma((ITERS, nz)), dma((ITERS, nz)),
            dma((nz, 4)), dma((nz, 4)),
            dma,
        ],
        compiler_params=pltpu.CompilerParams(
            collective_id=0, has_side_effects=True, vmem_limit_bytes=48 * 1024 * 1024
        ),
    )(
        cells, footprints, marks, jnp.broadcast_to(ids[None], (8, lanes)), ids[:, None],
        place[:, None], jnp.broadcast_to(place[None], (8, place.shape[0])),
    )
    return feet, lax.dynamic_slice(
        marks, (lax.axis_index("ta") * local, 0), (local, owned))


def solution(mesh):
    placed = (
        P("ta", None, "ty", "tx"),
        P(("ty", "tx"), None),
        P("ta", ("ty", "tx")),
        P(("ty", "tx")),
        P(("ty", "tx")),
    )
    return jax.shard_map(
        shards,
        mesh=mesh,
        in_specs=placed,
        out_specs=(P(("ty", "tx"), None), P("ta", ("ty", "tx"))),
        check_vma=False,
    )
```

time: 574 us -> 157 us (0.27); the launches traced: 563 us -> 155 us
  local copies, waits for them, and re-layouts: 188 us -> 31.7 us
  waiting for transfers between devices: 143 us -> 0 us
  Pallas kernels: 0 us -> 122 us
  other arithmetic: 97.1 us -> 0.18 us
  starting transfers between devices: 50.5 us -> 0 us
  matrix products: 46.2 us -> 0 us
  blocking collectives: 22.5 us -> 0 us
  between operations: 15.3 us -> 0.75 us
    pallas_call x0 -> x1, Pallas kernels: none -> 122 us  [shards(): pl.pallas_call(functools.partial(kernel, (ny, nx, nz, rows, cols, local,...]
    psum x2 -> x0, waiting for transfers between devices: 85.5 us -> none  [shards(): numerator, strength = lax.psum((numer_part, strength_part), 'ta')]
    ppermute x20 -> x0, waiting for transfers between devices: 57.7 us -> none  [the longest x10 36.4 us: with_halo(): lax.ppermute(tail, axis, [(i, (i + 1) % count) for i in range(ends)])]
    unnamed x58 -> x11, local copies, waits for them, and re-layouts: 56.6 us -> 0.99 us
    ppermute x20 -> x0, starting transfers between devices: 50.4 us -> none  [the longest x10 36.5 us: with_halo(): lax.ppermute(tail, axis, [(i, (i + 1) % count) for i in range(ends)])]
    dot_general x4 -> x0, matrix products: 46.2 us -> none  [the longest x2 30.3 us: shards(): jnp.einsum('kse,ksfe->fk', shaped, gathered, precision=lax.Precision.HIGH...]
    scatter-add x20 -> x0, other arithmetic: 45.7 us -> none  [the longest x4 36.2 us: patch_residue(): jax.ops.segment_sum(products.reshape(owned * 4, -1), cell_ids, num_segmen...]
    slice x28 -> x0, local copies, waits for them, and re-layouts: 25.3 us -> none  [the longest x10 10.9 us: with_halo(): lax.slice_in_dim(cells, cells.shape[dim] - width, cells.shape[dim], axis=...]
  transfers between devices with their start and end apart: 22 -> 0, of which waited for: 11 -> 0; matrix products, arithmetic and copies ran while one was open for 15% -> 0% of each run, Pallas kernels for 0% -> 0%
where the time goes in v1:
time: 157 us; the launch traced here: 155 us
  Pallas kernels  122 us (78%)
  local copies, waits for them, and re-layouts  31.7 us (20%)
    pallas_call x1, Pallas kernels, shards(): pl.pallas_call(functools.partial(kernel, (ny, nx, nz, rows, cols, local,...  122 us
    reshape x2, local copies, waits for them, and re-layouts, shards(): movie.reshape(local, planes, rows, CELL, cols, CELL)  19.4 us
    reshape x1, local copies, waits for them, and re-layouts, shards(): cells = cells.reshape(planes, local, rows * cols, spot)  10.2 us

profile of v1, /device:TPU:0, one launch (start us, length us, event | category | flops | bytes accessed | tf_op | source)
XLA Modules:
  0.0 154.9 jit_solution(17413467803605766867)
XLA Ops:
  0.6 9.6 %reshape.179 = bf16[4,4,16,16,8,16]{5,4,3,2,1,0:T(8,128)(2,1)} reshape(bf16[4,4,256,128]{3,2,1,0:T(8,128)(2,1)} %param.8) | data formatting | bytes 2097152 | tf_op jit(solution)/shard_map/reshape | solution.py:300
  10.2 9.8 %copy.30 = bf16[4,4,16,16,8,16]{5,3,4,2,0,1:T(8,128)(2,1)} copy(bf16[4,4,16,16,8,16]{5,4,3,2,1,0:T(8,128)(2,1)} %reshape.179) | data formatting | bytes 2097152 | tf_op jit(solution)/shard_map/reshape | solution.py:300
  20.0 0.0 copy-start.1
  20.0 0.0 copy-start.2
  20.0 0.0 copy-start.3
  20.0 0.0 copy-start.4
  20.0 0.0 copy-start
  20.0 10.2 %reshape.180.movie = bf16[4,4,128,256]{3,2,1,0:T(8,128)(2,1)S(1)} reshape(bf16[4,4,16,8,16,16]{5,4,3,2,1,0:T(8,128)(2,1)} %bitcast.15) | data formatting | bytes 2097152 | tf_op jit(solution)/shard_map/reshape | solution.py:301
  30.2 0.0 copy-done.1
  30.2 0.1 tile.10
  30.3 0.0 copy-done.2
  30.3 0.0 copy-done.3
  30.3 0.0 copy-done.4
  30.3 0.1 add_convert_fusion
  30.4 0.1 convert_element_type.37
  30.5 0.1 convert_element_type.41.idcol
  30.7 0.1 concatenate.36
  30.8 0.1 copy.28.place
  31.0 0.1 concatenate.37
  31.1 0.0 copy-done
  31.1 122.3 %shard_map.77 = (f32[64,4096]{1,0:T(8,128)S(1)}, f32[16,256]{1,0:T(8,128)S(1)}) custom-call(bf16[4,4,128,256]{3,2,1,0:T(8,128)(2,1)S(1)} %reshape.180.movie, f32[64,4096]{1,0:T(8,128)S(1)} %copy-done, f32[8,256]{1,0:T(8,128)S(1)} %scatter.4.trace, f32[8,256]{1,0:T(8,128)S(1)} %broadcast_in_dim.4.idrow, f32[256,1]{1,0:T(8,128)S(1)} %convert_element_type.41.idcol, ...), custom_call_target="tpu_custom_call" | custom-call | tf_op jit(solution)/shard_map/pallas_call | solution.py:328
  153.4 0.6 constant_dynamic-slice_fusion
  154.0 1.0 copy.32
  (13 shorter events, 0.1 us)
Async XLA Ops:
  20.0 10.2 %copy-start.1 = (f32[4,64]{1,0:T(4,128)S(1)}, f32[4,64]{1,0:T(4,128)}, u32[]{:S(2)}) copy-start(f32[4,64]{1,0:T(4,128)} %param.10) | copy-start | bytes 3076
  20.0 10.3 %copy-start.2 = (s32[64]{0:T(128)S(1)}, s32[64]{0:T(128)}, u32[]{:S(2)}) copy-start(s32[64]{0:T(128)} %param.12) | copy-start | bytes 772
  20.0 10.3 %copy-start.3 = (s32[64]{0:T(128)S(1)}, s32[64]{0:T(128)}, u32[]{:S(2)}) copy-start(s32[64]{0:T(128)} %param.11) | copy-start | bytes 772
  20.0 10.3 %copy-start.4 = (s32[4]{0:T(128)S(1)}, s32[4]{0:T(128)}, u32[]{:S(2)}) copy-start(s32[4]{0:T(128)} %constant.147.clone) | copy-start | bytes 52
  20.0 11.1 %copy-start = (f32[64,4096]{1,0:T(8,128)S(1)}, f32[64,4096]{1,0:T(8,128)}, u32[]{:S(2)}) copy-start(f32[64,4096]{1,0:T(8,128)} %foot.1) | copy-start | bytes 3145732

commit v2 on v1

--- a/solution.py
+++ b/solution.py
@@ -166,6 +166,20 @@
 
     for n in range(ITERS):
         feet = foot_at[n, 0]
+        def met_movie():
+            energy = nt(jnp.ones((8, spot), F32), feet * feet)
+
+            feet_t[...] = feet
+
+            def inner(f, carry):
+                numer[pl.ds(f, 1), :] = jnp.sum(
+                    jnp.transpose(feet_t[...] * patch[f]), axis=0, keepdims=True)
+                return carry
+            lax.fori_loop(0, frames, inner, 0)
+            return energy
+
+        if n:
+            energy = met_movie()
         update = jnp.zeros((frames, lanes), F32)
         same = []
         for j in range(slots):
@@ -217,15 +231,8 @@
                 patch[f] = got
                 return carry
             lax.fori_loop(0, frames, collect, 0)
-        energy = nt(jnp.ones((8, spot), F32), feet * feet)
-
-        feet_t[...] = feet
-
-        def inner(f, carry):
-            numer[pl.ds(f, 1), :] = jnp.sum(
-                jnp.transpose(feet_t[...] * patch[f]), axis=0, keepdims=True)
-            return carry
-        lax.fori_loop(0, frames, inner, 0)
+        if n == 0:
+            energy = met_movie()
         part_at[n, iz, 0:frames, :] = update + numer[...]
         part_at[n, iz, frames:frames + 8, :] = energy
         for o in range(1, nz):

time: 157 us -> 154 us (0.981)
  Pallas kernels: 122 us -> 119 us
    pallas_call x1, Pallas kernels: 122 us -> 119 us  [shards(): pl.pallas_call(functools.partial(kernel, (ny, nx, nz, rows, cols, local,...]
where the time goes in v2:
time: 154 us; the launch traced here: 152 us
  Pallas kernels  119 us (77%)
  local copies, waits for them, and re-layouts  31.7 us (21%)
    pallas_call x1, Pallas kernels, shards(): pl.pallas_call(functools.partial(kernel, (ny, nx, nz, rows, cols, local,...  119 us
    reshape x2, local copies, waits for them, and re-layouts, shards(): movie.reshape(local, planes, rows, CELL, cols, CELL)  19.4 us
    reshape x1, local copies, waits for them, and re-layouts, shards(): cells = cells.reshape(planes, local, rows * cols, spot)  10.2 us

profile of v2, /device:TPU:0, one launch (start us, length us, event | category | flops | bytes accessed | tf_op | source)
XLA Modules:
  0.0 152.0 jit_solution(11192977234831018946)
XLA Ops:
  0.6 9.6 %reshape.179 = bf16[4,4,16,16,8,16]{5,4,3,2,1,0:T(8,128)(2,1)} reshape(bf16[4,4,256,128]{3,2,1,0:T(8,128)(2,1)} %param.8) | data formatting | bytes 2097152 | tf_op jit(solution)/shard_map/reshape | solution.py:307
  10.2 9.8 %copy.30 = bf16[4,4,16,16,8,16]{5,3,4,2,0,1:T(8,128)(2,1)} copy(bf16[4,4,16,16,8,16]{5,4,3,2,1,0:T(8,128)(2,1)} %reshape.179) | data formatting | bytes 2097152 | tf_op jit(solution)/shard_map/reshape | solution.py:307
  20.0 0.0 copy-start.1
  20.0 0.0 copy-start.2
  20.0 0.0 copy-start.3
  20.0 0.0 copy-start.4
  20.0 0.0 copy-start
  20.0 10.2 %reshape.180.movie = bf16[4,4,128,256]{3,2,1,0:T(8,128)(2,1)S(1)} reshape(bf16[4,4,16,8,16,16]{5,4,3,2,1,0:T(8,128)(2,1)} %bitcast.15) | data formatting | bytes 2097152 | tf_op jit(solution)/shard_map/reshape | solution.py:308
  30.2 0.0 copy-done.1
  30.2 0.1 tile.10
  30.3 0.0 copy-done.2
  30.3 0.0 copy-done.3
  30.3 0.0 copy-done.4
  30.3 0.1 add_convert_fusion
  30.4 0.1 convert_element_type.37
  30.5 0.1 convert_element_type.41.idcol
  30.7 0.1 concatenate.36
  30.8 0.1 copy.28.place
  31.0 0.1 concatenate.37
  31.1 0.0 copy-done
  31.1 119.3 %shard_map.77 = (f32[64,4096]{1,0:T(8,128)S(1)}, f32[16,256]{1,0:T(8,128)S(1)}) custom-call(bf16[4,4,128,256]{3,2,1,0:T(8,128)(2,1)S(1)} %reshape.180.movie, f32[64,4096]{1,0:T(8,128)S(1)} %copy-done, f32[8,256]{1,0:T(8,128)S(1)} %scatter.4.trace, f32[8,256]{1,0:T(8,128)S(1)} %broadcast_in_dim.4.idrow, f32[256,1]{1,0:T(8,128)S(1)} %convert_element_type.41.idcol, ...), custom_call_target="tpu_custom_call" | custom-call | tf_op jit(solution)/shard_map/pallas_call | solution.py:335
  150.4 0.6 constant_dynamic-slice_fusion
  151.0 1.0 copy.32
  (13 shorter events, 0.1 us)
Async XLA Ops:
  20.0 10.2 %copy-start.1 = (f32[4,64]{1,0:T(4,128)S(1)}, f32[4,64]{1,0:T(4,128)}, u32[]{:S(2)}) copy-start(f32[4,64]{1,0:T(4,128)} %param.10) | copy-start | bytes 3076
  20.0 10.3 %copy-start.2 = (s32[64]{0:T(128)S(1)}, s32[64]{0:T(128)}, u32[]{:S(2)}) copy-start(s32[64]{0:T(128)} %param.12) | copy-start | bytes 772
  20.0 10.3 %copy-start.3 = (s32[64]{0:T(128)S(1)}, s32[64]{0:T(128)}, u32[]{:S(2)}) copy-start(s32[64]{0:T(128)} %param.11) | copy-start | bytes 772
  20.0 10.3 %copy-start.4 = (s32[4]{0:T(128)S(1)}, s32[4]{0:T(128)}, u32[]{:S(2)}) copy-start(s32[4]{0:T(128)} %constant.147.clone) | copy-start | bytes 52
  20.0 11.1 %copy-start = (f32[64,4096]{1,0:T(8,128)S(1)}, f32[64,4096]{1,0:T(8,128)}, u32[]{:S(2)}) copy-start(f32[64,4096]{1,0:T(8,128)} %foot.1) | copy-start | bytes 3145732
